TPU v7x, 256 devices: a whole 4x4x8 slice. The times are simulated.
256 devices in a mesh: row: 8 (over x, core), col: 16 (over z_lo, y), depth: 2 (over z_hi).
Axes of the slice: x: 4, y: 4, z: 8 (z_hi: 2, z_lo: 4; z = z_hi * 4 + z_lo), core: 2. Of those that a mesh axis runs over, the one named last changes fastest.
Arguments:
- activations: bfloat16 [2, 1024, 8192], P('depth', 'col', 'row'), may hold values from -6 to 6
- weight_tiles: bfloat16 [8, 16, 56, 128, 128], P('row', 'col'), may hold values from -0.09375 to 0.09375
- tile_rows: int32 [8, 16, 56], P('row', 'col'), may hold values from 0 to 7, as said below
- tile_cols: int32 [8, 16, 56], P('row', 'col'), may hold values from 0 to 13, as said below
- grad_out: bfloat16 [2, 1024, 28672], P('depth', 'row', 'col'), may hold values from -6 to 6
Outputs:
- output: bfloat16 [2, 1024, 28672], P('depth', 'row', 'col')
- grad_input: bfloat16 [2, 1024, 8192], P('depth', 'col', 'row')
- grad_tiles: float32 [8, 16, 56, 128, 128], P('row', 'col')
Inputs may be any that keep to these rules, and one draw needn't show every extreme that they name: For each block (i, j), the pairs (tile_rows[i, j, k], tile_cols[i, j, k]) over k are 56 distinct tiles of the block's 8 x 14 grid, in increasing order of tile_rows * 14 + tile_cols. `tile_cols`: drawn together with tile_rows, as stated there.
All inputs are finite; a program needn't handle non-finite values.
Results may differ from a plain program's by a relative error of at most 0.001.
Values may be sent and summed in bfloat16 or wider, within the bound.
A program may use at most 128 MiB of HBM per device.

v0:
```python
import math

import jax
import jax.numpy as jnp
from jax import lax
from jax.sharding import PartitionSpec as P

TILE_SIZE = 128


def kept_products(left, right, rows_here, cols_here, count_rows, count_cols):
    total_rows = left.shape[0]

    def one_block(left_part, right_part):
        part_rows = left_part.shape[0]
        left_kept = jnp.take(left_part.reshape(part_rows, count_rows, TILE_SIZE), rows_here, axis=1)
        right_kept = jnp.take(
            right_part.reshape(part_rows, count_cols, TILE_SIZE), cols_here, axis=1
        )
        return jnp.einsum("tkb,tkj->kbj", left_kept, right_kept, preferred_element_type=jnp.float32)

    block_size = 512
    steps_count = total_rows // block_size
    left_blocks = left.reshape(steps_count, block_size, left.shape[1])
    right_blocks = right.reshape(steps_count, block_size, right.shape[1])

    def add_block(carry, pair):
        return (carry + one_block(pair[0], pair[1]), None)

    start_value = jnp.zeros((rows_here.shape[0], TILE_SIZE, TILE_SIZE), jnp.float32)
    summed, unused = lax.scan(add_block, start_value, (left_blocks, right_blocks))
    return summed


def shards(activations, weight_tiles, tile_rows, tile_cols, grad_out):
    kept_weights = weight_tiles[0, 0]
    rows_here = tile_rows[0, 0]
    cols_here = tile_cols[0, 0]
    width_rows = activations.shape[2]
    width_cols = grad_out.shape[2]
    count_rows = width_rows // TILE_SIZE
    count_cols = width_cols // TILE_SIZE
    tile_grid = jnp.zeros((count_rows, count_cols, TILE_SIZE, TILE_SIZE), jnp.bfloat16)
    tile_grid = tile_grid.at[rows_here, cols_here].set(kept_weights)
    dense_block = tile_grid.transpose(0, 2, 1, 3).reshape(width_rows, width_cols)
    gathered = lax.all_gather(activations[0], "col", axis=0, tiled=True)
    group_tokens = gathered.shape[0]
    segment = gathered
    out_rows = lax.psum_scatter(
        jnp.dot(segment, dense_block, preferred_element_type=jnp.float32),
        "row",
        scatter_dimension=0,
        tiled=True,
    )
    output = out_rows.astype(jnp.bfloat16)[None]
    grad_tokens = lax.all_gather(grad_out[0], "row", axis=0, tiled=True)
    segment = grad_tokens
    input_rows = lax.psum_scatter(
        lax.dot_general(
            segment, dense_block, (((1,), (1,)), ((), ())), preferred_element_type=jnp.float32
        ),
        "col",
        scatter_dimension=0,
        tiled=True,
    )
    grad_input = input_rows.astype(jnp.bfloat16)[None]
    grad_scale = math.sqrt(group_tokens * lax.axis_size("depth"))
    local_grad = kept_products(gathered, grad_tokens, rows_here, cols_here, count_rows, count_cols)
    summed_grad = lax.psum(local_grad, "depth")
    grad_tiles = (summed_grad / grad_scale)[None, None]
    return (output, grad_input, grad_tiles)


def solution(mesh):
    placed = (
        P("depth", "col", "row"),
        P("row", "col", None, None, None),
        P("row", "col", None),
        P("row", "col", None),
        P("depth", "row", "col"),
    )
    return jax.shard_map(
        shards,
        mesh=mesh,
        in_specs=placed,
        out_specs=(
            P("depth", "row", "col"),
            P("depth", "col", "row"),
            P("row", "col", None, None, None),
        ),
        check_vma=False,
    )
```

profile of v0, /device:TPU:1, one launch (start us, length us, event | category | flops | bytes accessed | tf_op | source)
XLA Modules:
  0.0 533.8 jit_solution(8827608066837357147)
XLA Ops:
  7.2 0.0 all-gather.5.cloned.1.call-start
  7.2 0.7 all-gather.5.cloned.1.call-update
  7.9 0.0 all-gather.7.cloned.1.call-start
  7.9 0.7 all-gather.7.cloned.1.call-update
  8.6 0.0 all-reduce.2.cloned.1.call-start
  8.7 78.5 %all-gather.5.cloned.1.call-done = bf16[1,1024,1024]{2,1,0:T(8,128)(2,1)} async-done(((bf16[1,64,1024]{2,1,0:T(8,128)(2,1)}), bf16[1,1024,1024]{2,1,0:T(8,128)(2,1)}) %all-gather.5.cloned.1.call-update) | async-done | bytes 2097168 | tf_op jit(solution)/shard_map/all_gather | solution.py:46
  87.2 42.6 %all-gather.7.cloned.1.call-done = bf16[1,1024,1792]{2,1,0:T(8,128)(2,1)} async-done(((bf16[1,128,1792]{2,1,0:T(8,128)(2,1)}), bf16[1,1024,1792]{2,1,0:T(8,128)(2,1)}) %all-gather.7.cloned.1.call-update) | async-done | bytes 3670032 | tf_op jit(solution)/shard_map/all_gather | solution.py:56
  129.8 61.9 %while.11 = (s32[]{:T(128)}, f32[56,128,128]{2,1,0:T(8,128)}, s32[56]{0:T(128)}, bf16[2,512,1024]{2,1,0:T(8,128)(2,1)}, s32[56]{0:T(128)}, /*index=5*/bf16[2,512,1792]{2,1,0:T(8,128)(2,1)}, s32[]{:T(128)}, s32[]{:T(128)}) while((s32[]{:T(128)}, f32[56,128,128]{2,1,0:T(8,128)}, s32[56]{0:T(128)}, bf16[2,512,1024]{2,1,0:T(8,128)(2,1)}, ...), condition=%wide.region_4.5_spmd.clone, body=%wide.region_3.4_spmd.clone.sunk | while | flops 948702208 | bytes 68694328 | solution.py:31
  129.8 0.7 fusion.34
  130.5 1.6 constant_dynamic-slice_fusion.4
  132.1 2.3 copy.58
  134.4 2.9 copy.59
  137.3 5.2 gather_fusion
  142.5 1.3 constant_dynamic-slice_fusion.5
  143.8 0.5 copy.60
  144.4 0.7 copy.61
  145.1 0.0 copy-start.2
  145.1 0.0 copy-start.4
  145.1 5.2 gather_fusion.1
  150.3 0.0 copy-done.2
  150.3 0.0 copy-done.4
  150.4 9.9 %select_add_fusion.2 = f32[56,128,128]{2,1,0:T(8,128)} fusion(f32[56,128,128]{2,1,0:T(8,128)} %get-tuple-element.160, pred[]{:T(512)S(6)} %compare.13, bf16[56,512,128]{2,1,0:T(8,128)(2,1)} %gather_fusion, pred[56]{0:T(512)(128)(4,1)S(1)} %get-tuple-element.148, bf16[56,512,128]{2,1,0:T(8,128)(2,1)} %gather_fusion.1, ...), kind=kOutput, calls=%fused_computation.10.clone.1 | convolution fusion | flops 948699136 | bytes 22020208 | tf_op jit(solution)/shard_map/while/body/eval_jaxpr/tkb,tkj->kbj/dot_general | solution.py:20
  160.2 0.7 fusion.34
  160.9 1.6 constant_dynamic-slice_fusion.4
  162.5 2.3 copy.58
  164.9 2.9 copy.59
  167.8 5.2 gather_fusion
  173.0 1.3 constant_dynamic-slice_fusion.5
  174.3 0.5 copy.60
  174.8 0.7 copy.61
  175.5 0.0 copy-start.2
  175.5 0.0 copy-start.4
  175.5 5.2 gather_fusion.1
  180.8 0.0 copy-done.2
  180.8 0.0 copy-done.4
  180.8 10.9 %select_add_fusion.2 = f32[56,128,128]{2,1,0:T(8,128)} fusion(f32[56,128,128]{2,1,0:T(8,128)} %get-tuple-element.160, pred[]{:T(512)S(6)} %compare.13, bf16[56,512,128]{2,1,0:T(8,128)(2,1)} %gather_fusion, pred[56]{0:T(512)(128)(4,1)S(1)} %get-tuple-element.148, bf16[56,512,128]{2,1,0:T(8,128)(2,1)} %gather_fusion.1, ...), kind=kOutput, calls=%fused_computation.10.clone.1 | convolution fusion | flops 948699136 | bytes 22020208 | tf_op jit(solution)/shard_map/while/body/eval_jaxpr/tkb,tkj->kbj/dot_general | solution.py:20
  191.7 0.0 copy-start.3
  191.7 0.0 copy-start.5
  191.7 0.0 copy-start.1
  191.7 0.0 all-reduce.2.cloned.1.call-update
  191.8 0.2 reduce-scatter.7.cloned.1.call-start
  192.0 0.4 copy-done.3
  192.4 0.0 copy-done.5
  192.4 2.7 broadcast_in_dim.35
  195.2 0.0 copy-done.1
  195.2 9.4 %scatter_fusion = bf16[8,14,128,128]{3,2,1,0:T(8,128)(2,1)} fusion(bf16[8,14,128,128]{3,2,1,0:T(8,128)(2,1)} %broadcast_in_dim.35, s32[56]{0:T(128)S(1)} %fusion.28, bf16[56,128,128]{2,1,0:T(8,128)(2,1)S(1)} %bitcast.88), kind=kCustom, calls=%fused_computation.2 | custom fusion | bytes 5505472 | tf_op jit(solution)/shard_map/scatter | solution.py:44
  204.6 6.2 %copy.33 = bf16[8,128,14,128]{1,0,3,2:T(8,128)(2,1)} copy(bf16[8,128,14,128]{3,1,2,0:T(8,128)(2,1)} %bitcast.81) | data formatting | bytes 7340032 | tf_op jit(solution)/shard_map/transpose | solution.py:45
  210.8 9.1 %fusion.21 = f32[1024,1024]{0,1:T(8,128)} fusion(bf16[1,1024,1792]{2,1,0:T(8,128)(2,1)} %bitcast.83, bf16[224,8,8,128]{3,2,1,0:T(8,128)(2,1)} %bitcast.86), kind=kOutput, calls=%fused_computation.33 | convolution fusion | flops 3758096384 | bytes 11534336 | tf_op jit(solution)/shard_map/dot_general | solution.py:59
  219.9 5.3 %copy.39 = f32[1024,1024]{1,0:T(8,128)} copy(f32[1024,1024]{0,1:T(8,128)} %fusion.21) | data formatting | bytes 8388608
  225.3 0.0 copy-start
  225.3 0.0 reduce-scatter.7.cloned.1.call-update
  225.3 0.0 reduce-scatter.5.cloned.1.call-start
  225.3 1.5 copy-done
  226.9 8.1 %convolution_bitcast_fusion = f32[1024,1792]{0,1:T(8,128)} fusion(bf16[224,8,8,128]{3,2,1,0:T(8,128)(2,1)} %bitcast.87, bf16[1,1024,1024]{2,1,0:T(8,128)(2,1)S(1)} %bitcast.85), kind=kOutput, calls=%fused_computation.25 | convolution fusion | flops 3758096384 | bytes 13107200 | tf_op jit(solution)/shard_map/dot_general | solution.py:50
  235.0 0.0 reduce-scatter.5.cloned.1.call-update
  235.0 149.1 %all-reduce.2.cloned.1.call-done = f32[56,128,128]{2,1,0:T(8,128)} async-done(((f32[56,128,128]{2,1,0:T(8,128)}), f32[56,128,128]{2,1,0:T(8,128)}) %all-reduce.2.cloned.1.call-update) | async-done | bytes 3670032 | tf_op jit(solution)/shard_map/psum | solution.py:69
  384.1 4.5 multiply_bitcast_fusion
  388.6 78.2 %reduce-scatter.7.cloned.1.call-done = f32[64,1024]{1,0:T(8,128)} async-done(((f32[1024,1024]{1,0:T(8,128)}), f32[64,1024]{1,0:T(8,128)}) %reduce-scatter.7.cloned.1.call-update) | async-done | bytes 262160
  466.9 1.1 copy.40
  468.0 0.8 copy.37
  468.8 56.3 %reduce-scatter.5.cloned.1.call-done = f32[128,1792]{0,1:T(8,128)} async-done(((f32[1024,1792]{0,1:T(8,128)}), f32[128,1792]{0,1:T(8,128)}) %reduce-scatter.5.cloned.1.call-update) | async-done | bytes 917520 | tf_op jit(solution)/shard_map/reduce_scatter | solution.py:49
  525.1 1.2 convert_bitcast_fusion
  526.3 1.0 copy.36
  (8 shorter events, 0.1 us)
Async XLA Ops:
  7.2 80.0 %all-gather.5.cloned.1.call-start = ((), (), s32[]{:S(2)}) async-start(), calls=%async_computation.4 | async-start | bytes 2228224 | tf_op jit(solution)/shard_map/all_gather | solution.py:46
  7.9 121.9 %all-gather.7.cloned.1.call-start = ((), (), s32[]{:S(2)}) async-start(), calls=%async_computation.5 | async-start | bytes 4128768 | tf_op jit(solution)/shard_map/all_gather | solution.py:56
  8.6 375.5 %all-reduce.2.cloned.1.call-start = ((), (), s32[]{:S(2)}) async-start(), calls=%async_computation.3 | async-start | bytes 7340032 | tf_op jit(solution)/shard_map/psum | solution.py:69
  145.1 5.3 copy-start.2
  145.1 5.3 copy-start.4
  175.5 5.3 copy-start.2
  175.5 5.3 copy-start.4
  191.7 0.7 copy-start.3
  191.7 0.7 copy-start.5
  191.7 3.4 copy-start.1
  191.8 275.1 %reduce-scatter.7.cloned.1.call-start = ((), (), s32[]{:S(2)}) async-start(), calls=%async_computation.6 | async-start | bytes 4456448
  225.3 1.6 copy-start
  225.3 299.8 %reduce-scatter.5.cloned.1.call-start = ((), (), s32[]{:S(2)}) async-start(), calls=%async_computation.2 | async-start | bytes 8257536 | tf_op jit(solution)/shard_map/reduce_scatter | solution.py:49
Sparse Core Ops, SparseCore 0:
  9.8 77.3 all-gather.4
  89.0 40.7 all-gather.6
  191.9 192.2 all-reduce.1
  386.7 80.1 reduce-scatter.6
  469.4 55.6 reduce-scatter.4
where the time goes:
time: 535 us; the launch traced here: 534 us
  waiting for transfers between devices  406 us (76%)
  local copies, waits for them, and re-layouts  68.1 us (13%)
  matrix products  38.1 us (7%)
  between operations  13.8 us (3%)
  other arithmetic  7.11 us (1%)
    psum x1, waiting for transfers between devices, shards(): summed_grad = lax.psum(local_grad, 'depth')  149 us
    unnamed x6, waiting for transfers between devices  79.7 us
    all_gather x1, waiting for transfers between devices, shards(): gathered = lax.all_gather(activations[0], 'col', axis=0, tiled=True)  78.5 us
    reduce_scatter x1, waiting for transfers between devices, shards(): lax.psum_scatter(jnp.dot(segment, dense_block, preferred_element_type=jnp...  56.3 us
    all_gather x1, waiting for transfers between devices, shards(): grad_tokens = lax.all_gather(grad_out[0], 'row', axis=0, tiled=True)  42.6 us
    dot_general x2, matrix products, one_block(): jnp.einsum('tkb,tkj->kbj', left_kept, right_kept, preferred_element_type=...  20.8 us
    dynamic_slice x8, local copies, waits for them, and re-layouts, kept_products(): lax.scan(add_block, start_value, (left_blocks, right_blocks))  11.6 us
  transfers between devices with their start and end apart: 5, of which 5 were waited for; matrix products, arithmetic and copies ran while one was open for 9% of the time, Pallas kernels for 0%

commit v1 on v0

v1 whole, which is shorter than its diff:
```python
import functools
import math

import jax
import jax.numpy as jnp
from jax import lax
from jax.experimental import pallas as pl
from jax.experimental.pallas import tpu as pltpu
from jax.sharding import PartitionSpec as P

MESH = pl.DeviceIdType.MESH
T = 128
F32 = jnp.float32
NSEM = 128


def kernel(
    act, wt, rows, cols, gout,
    y_out, dx_out, dw_out,
    xall, gall, xst, gst, tiles, wd, dwd, dwt,
    dpart, dra, drb, drc, drd, dsum, dmine, zrecv,
    ypart, pair, ya, yb, yc, yd,
    ss, rs, ls, zss, zrs,
):
    r, c, d = lax.axis_index("row"), lax.axis_index("col"), lax.axis_index("depth")
    x, k, y, zl = r // 2, r % 2, c % 4, c // 4
    z = d * 4 + zl
    od = 1 - d

    def dev(dx=0, dk=0, dy=0, dz=0):
        zz = (z + dz + 8) % 8
        return {
            "row": ((x + dx + 4) % 4) * 2 + (k + dk) % 2,
            "col": (zz % 4) * 4 + (y + dy + 4) % 4,
            "depth": zz // 4,
        }

    def xs(zz, yy, lo=0, n=64):
        return xall.at[pl.ds(pl.multiple_of((zz * 4 + yy) * 64 + lo, 32), n)]

    def gs(dd, xx, kk, lo=0, n=128):
        return gall.at[pl.ds(pl.multiple_of(dd * 1024 + (xx * 2 + kk) * 128 + lo, 64), n)]

    zm = [(z + j + 8) % 8 for j in range(-4, 5)]
    zat = lambda j: zm[j + 4]
    yat = lambda j: (y + j + 4) % 4
    xat = lambda j: (x + j + 4) % 4

    ids = {}
    sent = {}

    def sem(name):
        if name not in ids:
            ids[name] = len(ids)
        return ids[name]

    def desc(name, src, dst, device):
        i = sem(name)
        return pltpu.make_async_remote_copy(
            src, dst, ss.at[i], rs.at[i], device_id=device, device_id_type=MESH
        )

    def send(name, make):
        desc(name, *make()).start()
        sent.setdefault(name, make)

    def recv(name, ref):
        desc(name, ref, ref, dev(dk=1)).wait_recv()

    local = [
        pltpu.make_async_copy(act.at[0], xs(z, y), ls.at[0]),
        pltpu.make_async_copy(gout.at[0], gs(d, x, k), ls.at[1]),
        pltpu.make_async_copy(wt.at[0, 0], tiles.at[pl.ds(0, 56)], ls.at[2]),
    ]
    for cp in local:
        cp.start()

    barrier = pltpu.get_barrier_semaphore()
    peers = [dev(dx=1), dev(dx=-1), dev(dk=1), dev(dy=1), dev(dy=-1)]
    peers += [dev(dz=j) for j in range(1, 8)]
    for peer in peers:
        pl.semaphore_signal(barrier, inc=1, device_id=peer, device_id_type=MESH)
    pl.semaphore_wait(barrier, len(peers))

    def z_send(h):
        if h < 3:
            up, down = zat(-h), zat(h)
            send(f"zu{h}", lambda: (act.at[0] if h == 0 else xs(up, y), xs(up, y), dev(dz=1)))
            send(f"zd{h}", lambda: (act.at[0] if h == 0 else xs(down, y), xs(down, y), dev(dz=-1)))
        else:
            send("zu3", lambda: (xs(zat(-3), y, 0, 32), xs(zat(-3), y, 0, 32), dev(dz=1)))
            send("zd3", lambda: (xs(zat(3), y, 32, 32), xs(zat(3), y, 32, 32), dev(dz=-1)))

    def z_recv(h):
        if h < 4:
            recv(f"zu{h - 1}", xs(zat(-h), y))
            recv(f"zd{h - 1}", xs(zat(h), y))
        else:
            recv("zu3", xs(zat(4), y, 0, 32))
            recv("zd3", xs(zat(4), y, 32, 32))

    def y_send(j, src=None):
        zz = zat(j)
        send(f"yu{j}", lambda: (xs(zz, y) if src is None else src, xs(zz, y), dev(dy=1)))
        send(f"yd{j}", lambda: (xs(zz, y) if src is None else src, xs(zz, y), dev(dy=-1)))

    def y_forward(j):
        zz = zat(j)
        recv(f"yu{j}", xs(zz, yat(-1)))
        send(f"yU{j}", lambda: (xs(zz, yat(-1), 0, 32), xs(zz, yat(-1), 0, 32), dev(dy=1)))
        recv(f"yd{j}", xs(zz, yat(1)))
        send(f"yD{j}", lambda: (xs(zz, yat(1), 32, 32), xs(zz, yat(1), 32, 32), dev(dy=-1)))

    def y_last(j):
        zz = zat(j)
        recv(f"yU{j}", xs(zz, yat(2), 0, 32))
        recv(f"yD{j}", xs(zz, yat(2), 32, 32))

    def both(h, own, do):
        if own:
            do(h)
            do(-h)

    def g_send(tag, dd, src):
        send(f"gk0{tag}", lambda: (src, gs(dd, x, k), dev(dk=1)))
        send(f"gu{tag}", lambda: (src, gs(dd, x, k), dev(dx=1)))
        send(f"gd{tag}", lambda: (src, gs(dd, x, k), dev(dx=-1)))

    def g_forward(tag, dd):
        left, right = xat(-1), xat(1)
        recv(f"gu{tag}", gs(dd, left, k))
        send(f"gU{tag}", lambda: (gs(dd, left, k, 0, 64), gs(dd, left, k, 0, 64), dev(dx=1)))
        send(f"gk1{tag}", lambda: (gs(dd, left, k), gs(dd, left, k), dev(dk=1)))
        recv(f"gd{tag}", gs(dd, right, k))
        send(f"gD{tag}", lambda: (gs(dd, right, k, 64, 64), gs(dd, right, k, 64, 64), dev(dx=-1)))
        send(f"gk3{tag}", lambda: (gs(dd, right, k), gs(dd, right, k), dev(dk=1)))

    def g_last(tag, dd):
        far = xat(2)
        recv(f"gU{tag}", gs(dd, far, k, 0, 64))
        recv(f"gD{tag}", gs(dd, far, k, 64, 64))
        send(f"gk2{tag}", lambda: (gs(dd, far, k), gs(dd, far, k), dev(dk=1)))

    def g_core(tag, dd, j):
        xx = {0: x, 1: xat(-1), 2: xat(2), 3: xat(1)}[j]
        recv(f"gk{j}{tag}", gs(dd, xx, 1 - k))

    def g_stage(j):
        base = pl.multiple_of(d * 1024 + xat(j) * 256, 256)
        return pltpu.make_async_copy(gall.at[pl.ds(base, 256)], gst[j % 4], ls.at[8 + j % 4])

    def dx_compute(j):
        g_stage(j).start()
        g_stage(j).wait()

        @pl.loop(0, 4)
        def _(n):
            cut = pl.ds(pl.multiple_of(n * 256, 256), 256)
            dpart[j % 4][:, cut] = lax.dot_general(
                gst[j % 4][...], wd[cut, :],
                (((1,), (1,)), ((), ())), preferred_element_type=F32,
            )

    def dblock(q, j, half):
        return dpart[q % 4].at[pl.ds(pl.multiple_of(yat(j) * 64, 64), 64), pl.ds(half * 512, 512)]

    def dx_send(j):
        p = xat(j)
        send(f"da{j}", lambda: (dblock(j, 2, 0), dra[j % 4], dev(dy=1)))
        send(f"db{j}", lambda: (dblock(j, 2, 1), drb[j % 4], dev(dy=-1)))
        send(f"dc1{j}", lambda: (dblock(j, 1, 1), drc[j % 4][1], dev(dy=1)))
        send(f"dd0{j}", lambda: (dblock(j, -1, 0), drd[j % 4][0], dev(dy=-1)))

    def dx_middle(j):
        p = xat(j)
        recv(f"da{j}", dra[j % 4])
        dra[j % 4][...] += dblock(j, 1, 0)[...]
        send(f"dc0{j}", lambda: (dra[j % 4], drc[j % 4][0], dev(dy=1)))
        recv(f"db{j}", drb[j % 4])
        drb[j % 4][...] += dblock(j, -1, 1)[...]
        send(f"dd1{j}", lambda: (drb[j % 4], drd[j % 4][1], dev(dy=-1)))

    def dx_last(j):
        p = xat(j)
        for half in (1, 0):
            recv(f"dc{half}{j}", drc[j % 4][half])
            recv(f"dd{1 - half}{j}", drd[j % 4][1 - half])
        for half in range(2):
            dsum[j % 4][:, half * 512:half * 512 + 512] = (
                dblock(j, 0, half)[...] + drc[j % 4][half][...] + drd[j % 4][half][...]
            )

        @pl.when(p == zl)
        def _():
            dmine[...] = dsum[j % 4][...]

        @pl.when(p != zl)
        def _():
            slot = (zl - p + 4) % 4 - 1
            pltpu.make_async_remote_copy(
                dsum[j % 4], zrecv.at[slot], zss.at[slot], zrs.at[slot],
                device_id={"row": r, "col": p * 4 + y, "depth": d}, device_id_type=MESH,
            ).start()

    def x_stage(j):
        base = pl.multiple_of(d * 1024 + xat(j) * 256, 256)
        return pltpu.make_async_copy(xall.at[pl.ds(base, 256)], xst[j % 4], ls.at[4 + j % 4])

    def y_compute(j):
        x_stage(j).wait()

        @pl.loop(0, 7)
        def _(n):
            cut = pl.ds(pl.multiple_of(n * 256, 256), 256)
            ypart[j % 4][:, cut] = jnp.dot(
                xst[j % 4][...], wd[:, cut], preferred_element_type=F32
            )

        send(f"p{j}", lambda: (ypart[j % 4].at[pl.ds(pl.multiple_of((1 - k) * 128, 128), 128)], pair[j % 4], dev(dk=1)))

    def yblock(j, half):
        return pair[j % 4].at[:, pl.ds(half * 896, 896)]

    def y_pair(j):
        recv(f"p{j}", pair[j % 4])
        pair[j % 4][...] += ypart[j % 4][pl.ds(pl.multiple_of(k * 128, 128), 128), :]

    local[2].wait()
    tiles[56] = jnp.zeros((T, T), jnp.bfloat16)

    g_send("o", d, gout.at[0])
    z_send(0)
    y_send(0, act.at[0])

    def fill(i, at):
        for j in range(14):
            cell = i * 14 + j
            here = jnp.minimum(at, 55)
            hit = jnp.logical_and(at < 56, rows[0, 0, here] * 14 + cols[0, 0, here] == cell)
            wd[pl.ds(pl.multiple_of(i * T, T), T), j * T:j * T + T] = tiles[jnp.where(hit, at, 56)]
            at = at + hit.astype(jnp.int32)
        return at

    lax.fori_loop(0, 8, fill, jnp.int32(0))

    z_recv(1)
    z_send(1)
    both(1, True, y_send)
    y_forward(0)
    local[1].wait()
    g_core("o", d, 0)
    dx_compute(0)
    z_recv(2)
    z_send(2)
    both(2, True, y_send)
    dx_send(0)
    both(1, True, y_forward)
    z_recv(3)
    z_send(3)
    both(3, True, y_send)
    send("gz0", lambda: (gout.at[0, pl.ds(0, 64)], gs(d, x, k, 0, 64), dev(dz=4)))
    send("gz1", lambda: (gout.at[0, pl.ds(64, 64)], gs(d, x, k, 64, 64), dev(dz=4)))
    both(2, True, y_forward)
    g_forward("o", d)
    both(3, True, y_forward)
    g_core("o", d, 1)
    dx_compute(-1)
    dx_send(-1)
    g_core("o", d, 3)
    dx_compute(1)
    dx_send(1)
    dx_middle(0)
    local[0].wait()
    y_last(0)
    for h in (1, 2, 3):
        both(h, True, y_last)
    for j in (2, 1, -1, 0):
        x_stage(j).start()
    y_compute(2)
    y_compute(1)
    y_pair(2)
    send("oa", lambda: (yblock(2, 0), ya, dev(dx=1)))
    send("ob", lambda: (yblock(2, 1), yb, dev(dx=-1)))
    y_compute(-1)
    y_pair(1)
    send("oc1", lambda: (yblock(1, 1), yc[1], dev(dx=1)))
    y_pair(-1)
    send("od0", lambda: (yblock(-1, 0), yd[0], dev(dx=-1)))
    g_last("o", d)
    g_core("o", d, 2)
    dx_compute(2)
    dx_send(2)
    z_recv(4)
    for h in (1, 2, 3):
        both(h, False, y_send)
    y_send(4)
    y_compute(0)
    recv("gz0", gs(od, x, k, 0, 64))
    recv("gz1", gs(od, x, k, 64, 64))
    g_send("t", od, gs(od, x, k))
    dx_middle(-1)
    dx_middle(1)
    recv("oa", ya)
    ya[...] += yblock(1, 0)[...]
    send("oc0", lambda: (ya, yc[0], dev(dx=1)))
    recv("ob", yb)
    yb[...] += yblock(-1, 1)[...]
    send("od1", lambda: (yb, yd[1], dev(dx=-1)))

    def dw_compute(dd, first):
        base = pl.multiple_of(dd * 1024, 1024)

        @pl.loop(0, 7)
        def _(n):
            cut = pl.ds(pl.multiple_of(n * 256, 256), 256)
            got = lax.dot_general(
                xall[pl.ds(base, 1024), :], gall[pl.ds(base, 1024), cut],
                (((0,), (0,)), ((), ())), preferred_element_type=F32,
            )
            for i in range(8):
                for j in range(2):
                    part = got[i * T:i * T + T, j * T:j * T + T]
                    at = i * 14 + n * 2 + j
                    dwd[at] = part if first else dwd[at] + part

    dx_last(0)
    dw_compute(d, True)
    dx_middle(2)
    dx_last(-1)
    dx_last(1)
    for h in (1, 2, 3):
        both(h, False, y_forward)
    y_forward(4)
    g_forward("t", od)
    dx_last(2)
    y_pair(0)
    g_last("t", od)
    for h in (1, 2, 3):
        both(h, False, y_last)
    y_last(4)
    for j in range(4):
        g_core("t", od, j)
    dw_compute(od, False)

    scale = 1.0 / math.sqrt(2048.0)

    @pl.loop(0, 8)
    def _(n):
        for i in range(7):
            t = n * 7 + i
            dwt[t] = dwd[rows[0, 0, t] * 14 + cols[0, 0, t]] * scale

    out = pltpu.make_async_copy(dwt, dw_out.at[0, 0], ls.at[3])
    out.start()
    for half in range(2):
        recv(f"oc{1 - half}", yc[1 - half])
        recv(f"od{half}", yd[half])
    for half in range(2):
        y_out[0, :, half * 896:half * 896 + 896] = (
            yblock(0, half)[...] + yc[half][...] + yd[half][...]
        ).astype(jnp.bfloat16)
    for slot in range(3):
        pltpu.make_async_remote_copy(
            zrecv.at[slot], zrecv.at[slot], zss.at[slot], zrs.at[slot],
            device_id=dev(dk=1), device_id_type=MESH,
        ).wait()
    dx_out[0] = (dmine[...] + zrecv[0] + zrecv[1] + zrecv[2]).astype(jnp.bfloat16)
    out.wait()
    for name, make in sent.items():
        desc(name, *make()).wait_send()


def shards(act, wt, rows, cols, gout):
    hbm = pl.BlockSpec(memory_space=pl.ANY)
    smem = pl.BlockSpec(memory_space=pltpu.SMEM)
    vmem = pl.BlockSpec(memory_space=pltpu.VMEM)
    bf16 = jnp.bfloat16
    dma = pltpu.SemaphoreType.DMA
    return tuple(
        pl.pallas_call(
            kernel,
            out_shape=[
                jax.ShapeDtypeStruct((1, 128, 1792), bf16),
                jax.ShapeDtypeStruct((1, 64, 1024), bf16),
                jax.ShapeDtypeStruct((1, 1, 56, T, T), F32),
            ],
            in_specs=[hbm, hbm, smem, smem, hbm],
            out_specs=[vmem, vmem, hbm],
            scratch_shapes=[
                pltpu.VMEM((2048, 1024), bf16),
                pltpu.VMEM((2048, 1792), bf16),
                [pltpu.VMEM((256, 1024), bf16)] * 4,
                [pltpu.VMEM((256, 1792), bf16)] * 4,
                pltpu.VMEM((57, T, T), bf16),
                pltpu.VMEM((1024, 1792), bf16),
                pltpu.VMEM((112, T, T), F32),
                pltpu.VMEM((56, T, T), F32),
                [pltpu.VMEM((256, 1024), F32)] * 4,
                [pltpu.VMEM((64, 512), F32)] * 4,
                [pltpu.VMEM((64, 512), F32)] * 4,
                [[pltpu.VMEM((64, 512), F32)] * 2] * 4,
                [[pltpu.VMEM((64, 512), F32)] * 2] * 4,
                [pltpu.VMEM((64, 1024), F32)] * 4,
                pltpu.VMEM((64, 1024), F32),
                pltpu.VMEM((3, 64, 1024), F32),
                [pltpu.VMEM((256, 1792), F32)] * 4,
                [pltpu.VMEM((128, 1792), F32)] * 4,
                pltpu.VMEM((128, 896), F32),
                pltpu.VMEM((128, 896), F32),
                [pltpu.VMEM((128, 896), F32)] * 2,
                [pltpu.VMEM((128, 896), F32)] * 2,
                dma((NSEM,)), dma((NSEM,)), dma((12,)), dma((3,)), dma((3,)),
            ],
            compiler_params=pltpu.CompilerParams(
                collective_id=0, has_side_effects=True, vmem_limit_bytes=62 * 2**20
            ),
        )(act, wt, rows, cols, gout)
    )


def solution(mesh):
    placed = (
        P("depth", "col", "row"),
        P("row", "col", None, None, None),
        P("row", "col", None),
        P("row", "col", None),
        P("depth", "row", "col"),
    )
    return jax.shard_map(
        shards,
        mesh=mesh,
        in_specs=placed,
        out_specs=(
            P("depth", "row", "col"),
            P("depth", "col", "row"),
            P("row", "col", None, None, None),
        ),
        check_vma=False,
    )
```

time: 535 us -> 125 us (0.23)
  waiting for transfers between devices: 406 us -> 0 us
  Pallas kernels: 0 us -> 116 us
  local copies, waits for them, and re-layouts: 68.1 us -> 7.68 us
  matrix products: 38.1 us -> 0 us
  between operations: 13.8 us -> 0.64 us
  other arithmetic: 7.11 us -> 0 us
    psum x1 -> x0, waiting for transfers between devices: 149 us -> none  [shards(): summed_grad = lax.psum(local_grad, 'depth')]
    all_gather x2 -> x0, waiting for transfers between devices: 121 us -> none  [the longest x1 78.5 us: shards(): gathered = lax.all_gather(activations[0], 'col', axis=0, tiled=True)]
    pallas_call x0 -> x1, Pallas kernels: none -> 116 us  [shards(): pl.pallas_call(kernel, out_shape=[jax.ShapeDtypeStruct((1, 128, 1792), bf...]
    unnamed x6 -> x0, waiting for transfers between devices: 79.7 us -> none
    reduce_scatter x1 -> x0, waiting for transfers between devices: 56.3 us -> none  [shards(): lax.psum_scatter(jnp.dot(segment, dense_block, preferred_element_type=jnp...]
    dot_general x4 -> x0, matrix products: 38.1 us -> none  [the longest x2 20.8 us: one_block(): jnp.einsum('tkb,tkj->kbj', left_kept, right_kept, preferred_element_type=...]
    gather x4 -> x0, local copies, waits for them, and re-layouts: 20.9 us -> none  [the longest x2 10.5 us: one_block(): jnp.take(left_part.reshape(part_rows, count_rows, TILE_SIZE), rows_here,...]
    dynamic_slice x8 -> x0, local copies, waits for them, and re-layouts: 11.6 us -> none  [kept_products(): lax.scan(add_block, start_value, (left_blocks, right_blocks))]
  transfers between devices with their start and end apart: 5 -> 0, of which waited for: 5 -> 0; matrix products, arithmetic and copies ran while one was open for 9% -> 0% of each run, Pallas kernels for 0% -> 0%
where the time goes in v1:
time: 125 us
  Pallas kernels  116 us (93%)
  local copies, waits for them, and re-layouts  7.68 us (6%)
    pallas_call x1, Pallas kernels, shards(): pl.pallas_call(kernel, out_shape=[jax.ShapeDtypeStruct((1, 128, 1792), bf...  116 us
    unnamed x3, local copies, waits for them, and re-layouts  7.68 us

profile of v1, /device:TPU:1, one launch (start us, length us, event | category | flops | bytes accessed | tf_op | source)
XLA Modules:
  0.0 124.6 jit_solution(1734926009084591878)
XLA Ops:
  0.6 116.3 %shard_map.76 = (bf16[1,128,1792]{2,1,0:T(8,128)(2,1)}, bf16[1,64,1024]{2,1,0:T(8,128)(2,1)}, f32[1,1,56,128,128]{4,3,2,1,0:T(8,128)}) custom-call(bf16[1,64,1024]{2,1,0:T(8,128)(2,1)} %act.1, bf16[1,1,56,128,128]{4,3,2,1,0:T(8,128)(2,1)} %wt.1, s32[1,1,56]{2,1,0:T(1,128)} %rows.1, s32[1,1,56]{2,1,0:T(1,128)} %cols.1, bf16[1,128,1792]{2,1,0:T(8,128)(2,1)} %gout.1), custom_call_target="tpu_custom_call" | custom-call | tf_op jit(solution)/shard_map/pallas_call | solution.py:380
  117.0 1.8 %copy.11 = bf16[1,128,1792]{2,1,0:T(8,128)(2,1)} copy(bf16[1,128,1792]{2,1,0:T(8,128)(2,1)} %get-tuple-element.6) | data formatting | bytes 917504
  118.8 1.6 %copy.12 = bf16[1,64,1024]{2,1,0:T(8,128)(2,1)} copy(bf16[1,64,1024]{2,1,0:T(8,128)(2,1)} %get-tuple-element.7) | data formatting | bytes 262144
  120.3 4.3 %copy.13 = f32[1,1,56,128,128]{4,3,2,1,0:T(8,128)} copy(f32[1,1,56,128,128]{4,3,2,1,0:T(8,128)} %get-tuple-element.8) | data formatting | bytes 7340032

commit v2 on v1

--- a/solution.py
+++ b/solution.py
@@ -117,9 +117,11 @@
         recv(f"yD{j}", xs(zz, yat(2), 32, 32))
 
     def both(h, own, do):
-        if own:
-            do(h)
-            do(-h)
+        up, down = zl + h < 4, zl - h >= 0
+        if not own:
+            up, down = jnp.logical_not(up), jnp.logical_not(down)
+        pl.when(up)(lambda: do(h))
+        pl.when(down)(lambda: do(-h))
 
     def g_send(tag, dd, src):
         send(f"gk0{tag}", lambda: (src, gs(dd, x, k), dev(dk=1)))
@@ -242,6 +244,34 @@
         return at
 
     lax.fori_loop(0, 8, fill, jnp.int32(0))
+
+    def dw_compute(dd, first):
+        base = pl.multiple_of(dd * 1024, 1024)
+
+        @pl.loop(0, 7)
+        def _(n):
+            cut = pl.ds(pl.multiple_of(n * 256, 256), 256)
+            got = lax.dot_general(
+                xall[pl.ds(base, 1024), :], gall[pl.ds(base, 1024), cut],
+                (((0,), (0,)), ((), ())), preferred_element_type=F32,
+            )
+            for i in range(8):
+                for j in range(2):
+                    part = got[i * T:i * T + T, j * T:j * T + T]
+                    at = i * 14 + n * 2 + j
+                    dwd[at] = part if first else dwd[at] + part
+
+    def out_send():
+        send("oa", lambda: (yblock(2, 0), ya, dev(dx=1)))
+        send("ob", lambda: (yblock(2, 1), yb, dev(dx=-1)))
+
+    def out_middle():
+        recv("oa", ya)
+        ya[...] += yblock(1, 0)[...]
+        send("oc0", lambda: (ya, yc[0], dev(dx=1)))
+        recv("ob", yb)
+        yb[...] += yblock(-1, 1)[...]
+        send("od1", lambda: (yb, yd[1], dev(dx=-1)))
 
     z_recv(1)
     z_send(1)
@@ -253,23 +283,23 @@
     z_recv(2)
     z_send(2)
     both(2, True, y_send)
-    dx_send(0)
     both(1, True, y_forward)
     z_recv(3)
     z_send(3)
     both(3, True, y_send)
+    dx_send(0)
     send("gz0", lambda: (gout.at[0, pl.ds(0, 64)], gs(d, x, k, 0, 64), dev(dz=4)))
     send("gz1", lambda: (gout.at[0, pl.ds(64, 64)], gs(d, x, k, 64, 64), dev(dz=4)))
     both(2, True, y_forward)
     g_forward("o", d)
-    both(3, True, y_forward)
     g_core("o", d, 1)
     dx_compute(-1)
-    dx_send(-1)
     g_core("o", d, 3)
     dx_compute(1)
+    both(3, True, y_forward)
+    dx_middle(0)
+    dx_send(-1)
     dx_send(1)
-    dx_middle(0)
     local[0].wait()
     y_last(0)
     for h in (1, 2, 3):
@@ -279,8 +309,7 @@
     y_compute(2)
     y_compute(1)
     y_pair(2)
-    send("oa", lambda: (yblock(2, 0), ya, dev(dx=1)))
-    send("ob", lambda: (yblock(2, 1), yb, dev(dx=-1)))
+    out_send()
     y_compute(-1)
     y_pair(1)
     send("oc1", lambda: (yblock(1, 1), yc[1], dev(dx=1)))
@@ -300,44 +329,22 @@
     g_send("t", od, gs(od, x, k))
     dx_middle(-1)
     dx_middle(1)
-    recv("oa", ya)
-    ya[...] += yblock(1, 0)[...]
-    send("oc0", lambda: (ya, yc[0], dev(dx=1)))
-    recv("ob", yb)
-    yb[...] += yblock(-1, 1)[...]
-    send("od1", lambda: (yb, yd[1], dev(dx=-1)))
-
-    def dw_compute(dd, first):
-        base = pl.multiple_of(dd * 1024, 1024)
-
-        @pl.loop(0, 7)
-        def _(n):
-            cut = pl.ds(pl.multiple_of(n * 256, 256), 256)
-            got = lax.dot_general(
-                xall[pl.ds(base, 1024), :], gall[pl.ds(base, 1024), cut],
-                (((0,), (0,)), ((), ())), preferred_element_type=F32,
-            )
-            for i in range(8):
-                for j in range(2):
-                    part = got[i * T:i * T + T, j * T:j * T + T]
-                    at = i * 14 + n * 2 + j
-                    dwd[at] = part if first else dwd[at] + part
-
-    dx_last(0)
     dw_compute(d, True)
-    dx_middle(2)
-    dx_last(-1)
-    dx_last(1)
     for h in (1, 2, 3):
         both(h, False, y_forward)
     y_forward(4)
+    dx_middle(2)
+    dx_last(0)
+    dx_last(-1)
+    dx_last(1)
+    out_middle()
     g_forward("t", od)
     dx_last(2)
-    y_pair(0)
-    g_last("t", od)
     for h in (1, 2, 3):
         both(h, False, y_last)
     y_last(4)
+    y_pair(0)
+    g_last("t", od)
     for j in range(4):
         g_core("t", od, j)
     dw_compute(od, False)
@@ -370,20 +377,37 @@
         desc(name, *make()).wait_send()
 
 
+def hand_over(y_in, dx_in, dw_in, y_out, dx_out, dw_out, y_mid, dx_mid, dw_mid, sem):
+    steps = [(y_in, y_mid, y_out), (dx_in, dx_mid, dx_out)]
+    for i in range(4):
+        cut = pl.ds(i * 14, 14)
+        steps.append((dw_in.at[0, 0, cut], dw_mid.at[cut], dw_out.at[0, 0, cut]))
+    into = [pltpu.make_async_copy(a, b, sem.at[0, i]) for i, (a, b, c) in enumerate(steps)]
+    out = [pltpu.make_async_copy(b, c, sem.at[1, i]) for i, (a, b, c) in enumerate(steps)]
+    for cp in into:
+        cp.start()
+    for first, second in zip(into, out):
+        first.wait()
+        second.start()
+    for cp in out:
+        cp.wait()
+
+
 def shards(act, wt, rows, cols, gout):
     hbm = pl.BlockSpec(memory_space=pl.ANY)
     smem = pl.BlockSpec(memory_space=pltpu.SMEM)
     vmem = pl.BlockSpec(memory_space=pltpu.VMEM)
     bf16 = jnp.bfloat16
     dma = pltpu.SemaphoreType.DMA
-    return tuple(
+    outs = [
+        jax.ShapeDtypeStruct((1, 128, 1792), bf16),
+        jax.ShapeDtypeStruct((1, 64, 1024), bf16),
+        jax.ShapeDtypeStruct((1, 1, 56, T, T), F32),
+    ]
+    results = tuple(
         pl.pallas_call(
             kernel,
-            out_shape=[
-                jax.ShapeDtypeStruct((1, 128, 1792), bf16),
-                jax.ShapeDtypeStruct((1, 64, 1024), bf16),
-                jax.ShapeDtypeStruct((1, 1, 56, T, T), F32),
-            ],
+            out_shape=outs,
             in_specs=[hbm, hbm, smem, smem, hbm],
             out_specs=[vmem, vmem, hbm],
             scratch_shapes=[
@@ -416,6 +440,21 @@
             ),
         )(act, wt, rows, cols, gout)
     )
+    return tuple(
+        pl.pallas_call(
+            hand_over,
+            out_shape=outs,
+            in_specs=[hbm] * 3,
+            out_specs=[hbm] * 3,
+            scratch_shapes=[
+                pltpu.VMEM((1, 128, 1792), bf16),
+                pltpu.VMEM((1, 64, 1024), bf16),
+                pltpu.VMEM((56, T, T), F32),
+                dma((2, 6)),
+            ],
+            compiler_params=pltpu.CompilerParams(vmem_limit_bytes=60 * 2**20),
+        )(*results)
+    )
 
 
 def solution(mesh):

time: 125 us -> 111 us (0.89)
  local copies, waits for them, and re-layouts: 7.68 us -> 0 us
  Pallas kernels: 116 us -> 111 us
    unnamed x3 -> x0, local copies, waits for them, and re-layouts: 7.68 us -> none
    pallas_call x1 -> x2, Pallas kernels: 116 us -> 111 us  [the longest x1 107 us: shards(): pl.pallas_call(kernel, out_shape=outs, in_specs=[hbm, hbm, smem, smem, hb...]
where the time goes in v2:
time: 111 us
  Pallas kernels  111 us (100%)
    pallas_call x1, Pallas kernels, shards(): pl.pallas_call(kernel, out_shape=outs, in_specs=[hbm, hbm, smem, smem, hb...  107 us
    pallas_call x1, Pallas kernels, shards(): pl.pallas_call(hand_over, out_shape=outs, in_specs=[hbm] * 3, out_specs=[...  3.74 us

profile of v2, /device:TPU:1, one launch (start us, length us, event | category | flops | bytes accessed | tf_op | source)
XLA Modules:
  0.0 111.3 jit_solution(14315345104266937173)
XLA Ops:
  0.6 106.9 %shard_map.76 = (bf16[1,128,1792]{2,1,0:T(8,128)(2,1)}, bf16[1,64,1024]{2,1,0:T(8,128)(2,1)}, f32[1,1,56,128,128]{4,3,2,1,0:T(8,128)}) custom-call(bf16[1,64,1024]{2,1,0:T(8,128)(2,1)} %act.1, bf16[1,1,56,128,128]{4,3,2,1,0:T(8,128)(2,1)} %wt.1, s32[1,1,56]{2,1,0:T(1,128)} %rows.1, s32[1,1,56]{2,1,0:T(1,128)} %cols.1, bf16[1,128,1792]{2,1,0:T(8,128)(2,1)} %gout.1), custom_call_target="tpu_custom_call" | custom-call | tf_op jit(solution)/shard_map/pallas_call | solution.py:408
  107.5 3.7 %shard_map.77 = (bf16[1,128,1792]{2,1,0:T(8,128)(2,1)}, bf16[1,64,1024]{2,1,0:T(8,128)(2,1)}, f32[1,1,56,128,128]{4,3,2,1,0:T(8,128)}) custom-call(bf16[1,128,1792]{2,1,0:T(8,128)(2,1)} %get-tuple-element.6.y_in, bf16[1,64,1024]{2,1,0:T(8,128)(2,1)} %get-tuple-element.7.dx_in, f32[1,1,56,128,128]{4,3,2,1,0:T(8,128)} %get-tuple-element.8.dw_in), custom_call_target="tpu_custom_call" | custom-call | tf_op jit(solution)/shard_map/pallas_call | solution.py:444

commit v3 on v2

--- a/solution.py
+++ b/solution.py
@@ -330,15 +330,15 @@
     dx_middle(-1)
     dx_middle(1)
     dw_compute(d, True)
+    out_middle()
     for h in (1, 2, 3):
         both(h, False, y_forward)
     y_forward(4)
     dx_middle(2)
+    g_forward("t", od)
     dx_last(0)
     dx_last(-1)
     dx_last(1)
-    out_middle()
-    g_forward("t", od)
     dx_last(2)
     for h in (1, 2, 3):
         both(h, False, y_last)

time: 111 us -> 109 us (0.982)
  Pallas kernels: 111 us -> 108 us
    pallas_call x1, Pallas kernels: 107 us -> 104 us  [shards(): pl.pallas_call(kernel, out_shape=outs, in_specs=[hbm, hbm, smem, smem, hb...]
where the time goes in v3:
time: 109 us
  Pallas kernels  108 us (99%)
    pallas_call x1, Pallas kernels, shards(): pl.pallas_call(kernel, out_shape=outs, in_specs=[hbm, hbm, smem, smem, hb...  104 us
    pallas_call x1, Pallas kernels, shards(): pl.pallas_call(hand_over, out_shape=outs, in_specs=[hbm] * 3, out_specs=[...  3.74 us

profile of v3, /device:TPU:1, one launch (start us, length us, event | category | flops | bytes accessed | tf_op | source)
XLA Modules:
  0.0 108.8 jit_solution(10130294873203887765)
XLA Ops:
  0.6 104.4 %shard_map.76 = (bf16[1,128,1792]{2,1,0:T(8,128)(2,1)}, bf16[1,64,1024]{2,1,0:T(8,128)(2,1)}, f32[1,1,56,128,128]{4,3,2,1,0:T(8,128)}) custom-call(bf16[1,64,1024]{2,1,0:T(8,128)(2,1)} %act.1, bf16[1,1,56,128,128]{4,3,2,1,0:T(8,128)(2,1)} %wt.1, s32[1,1,56]{2,1,0:T(1,128)} %rows.1, s32[1,1,56]{2,1,0:T(1,128)} %cols.1, bf16[1,128,1792]{2,1,0:T(8,128)(2,1)} %gout.1), custom_call_target="tpu_custom_call" | custom-call | tf_op jit(solution)/shard_map/pallas_call | solution.py:408
  105.0 3.7 %shard_map.77 = (bf16[1,128,1792]{2,1,0:T(8,128)(2,1)}, bf16[1,64,1024]{2,1,0:T(8,128)(2,1)}, f32[1,1,56,128,128]{4,3,2,1,0:T(8,128)}) custom-call(bf16[1,128,1792]{2,1,0:T(8,128)(2,1)} %get-tuple-element.6.y_in, bf16[1,64,1024]{2,1,0:T(8,128)(2,1)} %get-tuple-element.7.dx_in, f32[1,1,56,128,128]{4,3,2,1,0:T(8,128)} %get-tuple-element.8.dw_in), custom_call_target="tpu_custom_call" | custom-call | tf_op jit(solution)/shard_map/pallas_call | solution.py:444

commit v4 on v3

--- a/solution.py
+++ b/solution.py
@@ -351,14 +351,14 @@
 
     scale = 1.0 / math.sqrt(2048.0)
 
-    @pl.loop(0, 8)
-    def _(n):
-        for i in range(7):
-            t = n * 7 + i
-            dwt[t] = dwd[rows[0, 0, t] * 14 + cols[0, 0, t]] * scale
-
-    out = pltpu.make_async_copy(dwt, dw_out.at[0, 0], ls.at[3])
-    out.start()
+    outs = []
+    for part in range(4):
+        for i in range(14):
+            t = part * 14 + i
+            dwt[part][i] = dwd[rows[0, 0, t] * 14 + cols[0, 0, t]] * scale
+        out = pltpu.make_async_copy(dwt[part], dw_out.at[0, 0, pl.ds(part * 14, 14)], ls.at[12 + part])
+        out.start()
+        outs.append(out)
     for half in range(2):
         recv(f"oc{1 - half}", yc[1 - half])
         recv(f"od{half}", yd[half])
@@ -372,7 +372,8 @@
             device_id=dev(dk=1), device_id_type=MESH,
         ).wait()
     dx_out[0] = (dmine[...] + zrecv[0] + zrecv[1] + zrecv[2]).astype(jnp.bfloat16)
-    out.wait()
+    for out in outs:
+        out.wait()
     for name, make in sent.items():
         desc(name, *make()).wait_send()
 
@@ -418,7 +419,7 @@
                 pltpu.VMEM((57, T, T), bf16),
                 pltpu.VMEM((1024, 1792), bf16),
                 pltpu.VMEM((112, T, T), F32),
-                pltpu.VMEM((56, T, T), F32),
+                [pltpu.VMEM((14, T, T), F32)] * 4,
                 [pltpu.VMEM((256, 1024), F32)] * 4,
                 [pltpu.VMEM((64, 512), F32)] * 4,
                 [pltpu.VMEM((64, 512), F32)] * 4,
@@ -433,7 +434,7 @@
                 pltpu.VMEM((128, 896), F32),
                 [pltpu.VMEM((128, 896), F32)] * 2,
                 [pltpu.VMEM((128, 896), F32)] * 2,
-                dma((NSEM,)), dma((NSEM,)), dma((12,)), dma((3,)), dma((3,)),
+                dma((NSEM,)), dma((NSEM,)), dma((16,)), dma((3,)), dma((3,)),
             ],
             compiler_params=pltpu.CompilerParams(
                 collective_id=0, has_side_effects=True, vmem_limit_bytes=62 * 2**20

time: 109 us -> 109 us (level)
  no operation moved by 1% of the time
where the time goes in v4:
time: 109 us; the launch traced here: 108 us
  Pallas kernels  108 us (99%)
    pallas_call x1, Pallas kernels, shards(): pl.pallas_call(kernel, out_shape=outs, in_specs=[hbm, hbm, smem, smem, hb...  104 us
    pallas_call x1, Pallas kernels, shards(): pl.pallas_call(hand_over, out_shape=outs, in_specs=[hbm] * 3, out_specs=[...  3.74 us

profile of v4, /device:TPU:1, one launch (start us, length us, event | category | flops | bytes accessed | tf_op | source)
XLA Modules:
  0.0 108.5 jit_solution(15860127550904918239)
XLA Ops:
  0.6 104.1 %shard_map.76 = (bf16[1,128,1792]{2,1,0:T(8,128)(2,1)}, bf16[1,64,1024]{2,1,0:T(8,128)(2,1)}, f32[1,1,56,128,128]{4,3,2,1,0:T(8,128)}) custom-call(bf16[1,64,1024]{2,1,0:T(8,128)(2,1)} %act.1, bf16[1,1,56,128,128]{4,3,2,1,0:T(8,128)(2,1)} %wt.1, s32[1,1,56]{2,1,0:T(1,128)} %rows.1, s32[1,1,56]{2,1,0:T(1,128)} %cols.1, bf16[1,128,1792]{2,1,0:T(8,128)(2,1)} %gout.1), custom_call_target="tpu_custom_call" | custom-call | tf_op jit(solution)/shard_map/pallas_call | solution.py:409
  104.7 3.7 %shard_map.77 = (bf16[1,128,1792]{2,1,0:T(8,128)(2,1)}, bf16[1,64,1024]{2,1,0:T(8,128)(2,1)}, f32[1,1,56,128,128]{4,3,2,1,0:T(8,128)}) custom-call(bf16[1,128,1792]{2,1,0:T(8,128)(2,1)} %get-tuple-element.6.y_in, bf16[1,64,1024]{2,1,0:T(8,128)(2,1)} %get-tuple-element.7.dx_in, f32[1,1,56,128,128]{4,3,2,1,0:T(8,128)} %get-tuple-element.8.dw_in), custom_call_target="tpu_custom_call" | custom-call | tf_op jit(solution)/shard_map/pallas_call | solution.py:445
